TPU v7x, 32 devices: a whole 2x2x4 slice. The times are simulated.
32 devices in a mesh: ctx: 8 (over z, y), tp: 4 (over x, core).
Axes of the slice: x: 2, y: 2, z: 4, core: 2. Of those that a mesh axis runs over, the one named last changes fastest.
Arguments:
- outer_gate: bfloat16 [1024, 1024], P('ctx', 'tp'), may hold values from -6 to 6
- inner_gate: bfloat16 [1024, 1024], P('ctx', 'tp'), may hold values from -6 to 6
- values: bfloat16 [1024, 1024], P('ctx', 'tp'), may hold values from -6 to 6
- residues: float32 [16, 1024], P(None, 'tp'), may hold values from -4 to 4
- log_decay: float32 [16, 1024], P(None, 'tp'), may hold values from -16 to -2, as said below
- skip_gain: float32 [1024], P('tp'), may hold values from 0.5 to 1.5
- out_weight: bfloat16 [1024, 8192], P('tp'), may hold values from -0.25 to 0.25
- out_grad: bfloat16 [1024, 8192], P('ctx', 'tp'), may hold values from -1.5 to 1.5
Outputs:
- mixed: bfloat16 [1024, 8192], P('ctx', 'tp')
- grad_outer: bfloat16 [1024, 1024], P('ctx', 'tp')
- grad_inner: bfloat16 [1024, 1024], P('ctx', 'tp')
- grad_values: bfloat16 [1024, 1024], P('ctx', 'tp')
- grad_weight: float32 [1024, 8192], P('tp', 'ctx')
- grad_skip: float32 [1024], P('tp')
- grad_residues: float32 [16, 1024], P(None, 'tp')
- grad_decay: float32 [16, 1024], P(None, 'tp')
Inputs may be any that keep to these rules, and one draw needn't show every extreme that they name: exp(log_decay) is a decay rate per position between 0.3 / 1024 and 0.12.
All inputs are finite; a program needn't handle non-finite values.
Results may differ from a plain program's by a relative error of at most 0.015.
Values may be sent and summed in bfloat16 or wider, within the bound.
A program may use at most 128 MiB of HBM per device.

v0:
```python
import math

import jax
import jax.numpy as jnp
from jax import lax
from jax.sharding import PartitionSpec as P

PRECISE = lax.Precision.HIGHEST


def for_sending(array):
    return jax.tree.map(lambda a: a.astype(jnp.bfloat16) if a.dtype == jnp.float32 else a, array)


def reversed_bits(position, levels):
    result = position * 0
    for bit_place in range(levels):
        result = result * 2 + position // 2**bit_place % 2
    return result


def rotate(stacked, cosine, sine_part):
    return jnp.stack(
        [
            stacked[:, 0] * cosine - stacked[:, 1] * sine_part,
            stacked[:, 0] * sine_part + stacked[:, 1] * cosine,
        ],
        axis=1,
    )


def square_table(length_dev, flip_sign):
    indices = jnp.arange(length_dev, dtype=jnp.int32)
    products = indices[:, None] * indices[None, :] % length_dev
    angles = flip_sign * 2.0 * math.pi / length_dev * products.astype(jnp.float32)
    return (jnp.cos(angles), jnp.sin(angles))


def local_transform(stacked, flip_sign):
    cosine, sine_part = square_table(stacked.shape[2], flip_sign)
    real_part = jnp.einsum("ki,sic->skc", cosine, stacked[:, 0], precision=PRECISE) - jnp.einsum(
        "ki,sic->skc", sine_part, stacked[:, 1], precision=PRECISE
    )
    imag_part = jnp.einsum("ki,sic->skc", cosine, stacked[:, 1], precision=PRECISE) + jnp.einsum(
        "ki,sic->skc", sine_part, stacked[:, 0], precision=PRECISE
    )
    return jnp.stack([real_part, imag_part], axis=1)


def shift_table(device, levels, length_dev, length, flip_sign):
    low_index = reversed_bits(device, levels)
    indices = jnp.arange(length_dev, dtype=jnp.int32)
    products = indices * low_index % length
    angles = flip_sign * 2.0 * math.pi / length * products.astype(jnp.float32)
    return (jnp.cos(angles)[:, None], jnp.sin(angles)[:, None])


def device_table(levels, forward):
    ctx_size = 2**levels
    indices = jnp.arange(ctx_size, dtype=jnp.int32)
    flipped = reversed_bits(indices, levels)
    if forward:
        products = flipped[:, None] * indices[None, :]
        flip_sign = -1.0
    else:
        products = indices[:, None] * flipped[None, :]
        flip_sign = 1.0
    angles = flip_sign * 2.0 * math.pi / ctx_size * (products % ctx_size).astype(jnp.float32)
    return (jnp.cos(angles), jnp.sin(angles))


def transpose_transform(stacked, tables):
    cosine, sine_part = tables
    shaped = stacked.reshape(stacked.shape[0], 2, 1, stacked.shape[2], stacked.shape[3])
    blocks = lax.all_to_all(
        for_sending(shaped), "ctx", split_axis=3, concat_axis=2, tiled=True
    ).astype(shaped.dtype)
    real_part = jnp.einsum("pq,sqic->spic", cosine, blocks[:, 0], precision=PRECISE) - jnp.einsum(
        "pq,sqic->spic", sine_part, blocks[:, 1], precision=PRECISE
    )
    imag_part = jnp.einsum("pq,sqic->spic", cosine, blocks[:, 1], precision=PRECISE) + jnp.einsum(
        "pq,sqic->spic", sine_part, blocks[:, 0], precision=PRECISE
    )
    combined = jnp.stack([real_part, imag_part], axis=1)
    result = lax.all_to_all(
        for_sending(combined), "ctx", split_axis=2, concat_axis=3, tiled=True
    ).astype(combined.dtype)
    return result.reshape(stacked.shape)


def branch_phase(device, length_dev, length, flip_sign):
    positions = (device * length_dev + jnp.arange(length_dev, dtype=jnp.int32)).astype(jnp.float32)
    angles = flip_sign * math.pi / length * positions
    return (jnp.cos(angles)[:, None], jnp.sin(angles)[:, None])


def to_spectrum(signals, device, levels, length, across):
    length_dev = signals.shape[1]
    cosine, sine_part = branch_phase(device, length_dev, length, -1.0)
    zero_part = jnp.zeros_like(signals)
    even_part = jnp.stack([signals, zero_part], axis=1)
    odd_part = jnp.stack([signals * cosine, signals * sine_part], axis=1)
    stacked = jnp.concatenate([even_part, odd_part], axis=0)
    stacked = across(stacked, True)
    cosine, sine_part = shift_table(device, levels, length_dev, length, -1.0)
    stacked = rotate(stacked, cosine, sine_part)
    return local_transform(stacked, -1.0)


def from_spectrum(stacked, device, levels, length, across):
    length_dev = stacked.shape[2]
    stacked = local_transform(stacked, 1.0)
    cosine, sine_part = shift_table(device, levels, length_dev, length, 1.0)
    stacked = rotate(stacked, cosine, sine_part)
    stacked = across(stacked, False)
    half_count = stacked.shape[0] // 2
    lower_half = stacked[:half_count]
    upper_half = stacked[half_count:]
    cosine, sine_part = branch_phase(device, length_dev, length, 1.0)
    summed = lower_half[:, 0] + upper_half[:, 0] * cosine - upper_half[:, 1] * sine_part
    return summed / (2.0 * length)


def filter_spectrum(residues, log_decay, device, levels, length):
    ctx_size = 2**levels
    length_dev = length // ctx_size
    rate_rows = jnp.exp(log_decay)
    gain_rows = residues * jnp.sqrt(-jnp.expm1(-2.0 * rate_rows))
    falloff = jnp.exp(-rate_rows)[:, None, :]
    tail_part = jnp.exp(-rate_rows * length)
    rim_term = (-jnp.expm1(-rate_rows))[:, None, :]
    low_index = reversed_bits(device, levels)
    indices = jnp.arange(length_dev, dtype=jnp.int32)
    filters = []
    for branch in range(2):
        frequency = 2 * (low_index + ctx_size * indices) + branch
        phases = math.pi / length * frequency.astype(jnp.float32)
        sine_theta = jnp.sin(phases)[None, :, None]
        half_sine = jnp.sin(0.5 * phases)[None, :, None]
        denom_real = rim_term + falloff * 2.0 * half_sine * half_sine
        denom_imag = falloff * sine_theta
        if branch == 0:
            numerator = gain_rows * (1.0 - tail_part)
        else:
            numerator = gain_rows * (1.0 + tail_part)
        weighting = numerator[:, None, :] / (denom_real * denom_real + denom_imag * denom_imag)
        real_part = jnp.sum(weighting * denom_real, axis=0)
        imag_part = -jnp.sum(weighting * denom_imag, axis=0)
        filters.append(jnp.stack([real_part, imag_part], axis=0))
    return filters


def multiply(left_factor, right_factor, conjugate):
    flip_sign = -1.0 if conjugate else 1.0
    right_imag = flip_sign * right_factor[1]
    return jnp.stack(
        [
            left_factor[0] * right_factor[0] - left_factor[1] * right_imag,
            left_factor[0] * right_imag + left_factor[1] * right_factor[0],
        ],
        axis=0,
    )


def filter_rows(residues, log_decay, positions):
    rate_rows = jnp.exp(log_decay)
    gain_rows = residues * jnp.sqrt(-jnp.expm1(-2.0 * rate_rows))
    return jnp.sum(
        gain_rows[:, None, :] * jnp.exp(-rate_rows[:, None, :] * positions[None, :, None]), axis=0
    )


def spectral_terms(mixed_in, grad_conv, residues, log_decay, device, levels, length, across):
    length_dev = mixed_in.shape[0]
    spectra = to_spectrum(jnp.stack([mixed_in, grad_conv], axis=0), device, levels, length, across)
    filters = filter_spectrum(residues, log_decay, device, levels, length)
    products = []
    for branch in range(2):
        spec_u = spectra[2 * branch]
        spec_g = spectra[2 * branch + 1]
        spec_h = filters[branch]
        products = products + [
            multiply(spec_u, spec_h, False),
            multiply(spec_g, spec_h, True),
            multiply(spec_g, spec_u, True),
        ]
    outcomes = from_spectrum(jnp.stack(products, axis=0), device, levels, length, across)
    positions = (device * length_dev + jnp.arange(length_dev, dtype=jnp.int32)).astype(jnp.float32)

    def local_rows(residue_part, decay_part):
        return filter_rows(residue_part, decay_part, positions)

    _, pullback = jax.vjp(local_rows, residues, log_decay)
    grad_res_part, grad_decay_part = pullback(outcomes[2])
    return (outcomes[0], outcomes[1], grad_res_part, grad_decay_part)


def body(outer_gate, inner_gate, values, residues, log_decay, skip_gain, out_weight, out_grad):
    ctx_size = lax.axis_size("ctx")
    device = lax.axis_index("ctx")
    levels = ctx_size.bit_length() - 1
    length_dev = outer_gate.shape[0]
    length = ctx_size * length_dev
    outer_f = outer_gate.astype(jnp.float32)
    inner_f = inner_gate.astype(jnp.float32)
    value_f = values.astype(jnp.float32)
    mixed_in = inner_f * value_f
    full_grad = lax.all_gather(out_grad, "tp", axis=1, tiled=True)
    grad_gated = lax.dot_general(
        full_grad, out_weight, (((1,), (1,)), ((), ())), preferred_element_type=jnp.float32
    )
    grad_conv = grad_gated * outer_f

    def across(stacked, forward):
        return transpose_transform(stacked, device_table(levels, forward))

    conv_out, corr_in, grad_res_part, grad_decay_part = spectral_terms(
        mixed_in, grad_conv, residues, log_decay, device, levels, length, across
    )
    gated = conv_out + skip_gain[None, :] * mixed_in
    result = (outer_f * gated).astype(jnp.bfloat16)
    proj_part = jnp.dot(result, out_weight, preferred_element_type=jnp.float32)
    mixed_out = lax.psum_scatter(
        proj_part.astype(jnp.bfloat16), "tp", scatter_dimension=1, tiled=True
    )
    weight_part = lax.dot_general(
        result, full_grad, (((0,), (0,)), ((), ())), preferred_element_type=jnp.float32
    )
    grad_weight = lax.psum_scatter(weight_part, "ctx", scatter_dimension=1, tiled=True)
    grad_outer = (grad_gated * gated).astype(jnp.bfloat16)
    grad_mixed = corr_in + skip_gain[None, :] * grad_conv
    grad_inner = (grad_mixed * value_f).astype(jnp.bfloat16)
    grad_values = (grad_mixed * inner_f).astype(jnp.bfloat16)
    skip_part = jnp.sum(grad_conv * mixed_in, axis=0)
    grad_skip, grad_residues, grad_decay = lax.psum(
        (skip_part, grad_res_part, grad_decay_part), "ctx"
    )
    return (
        mixed_out,
        grad_outer,
        grad_inner,
        grad_values,
        grad_weight,
        grad_skip,
        grad_residues,
        grad_decay,
    )


def solution(mesh):
    placed = (
        P("ctx", "tp"),
        P("ctx", "tp"),
        P("ctx", "tp"),
        P(None, "tp"),
        P(None, "tp"),
        P("tp"),
        P("tp", None),
        P("ctx", "tp"),
    )
    return jax.shard_map(
        body,
        mesh=mesh,
        in_specs=placed,
        out_specs=(
            P("ctx", "tp"),
            P("ctx", "tp"),
            P("ctx", "tp"),
            P("ctx", "tp"),
            P("tp", "ctx"),
            P("tp"),
            P(None, "tp"),
            P(None, "tp"),
        ),
        check_vma=False,
    )
```

profile of v0, /device:TPU:25, one launch (start us, length us, event | category | flops | bytes accessed | tf_op | source)
XLA Modules:
  0.0 335.4 jit_solution(16174796900705940159)
XLA Ops:
  7.2 0.7 all-gather.2.cloned.1.call-update
  8.0 0.9 fusion.52
  8.9 24.7 %all-gather.2.cloned.1.call-done = bf16[128,8192]{1,0:T(8,128)(2,1)} async-done(((bf16[128,2048]{1,0:T(8,128)(2,1)}), bf16[128,8192]{1,0:T(8,128)(2,1)}) %all-gather.2.cloned.1.call-update) | async-done | bytes 2097168 | tf_op jit(solution)/shard_map/all_gather | solution.py:208
  33.6 4.4 %fusion.196 = f32[128,256]{1,0:T(8,128)S(1)} fusion(bf16[128,8192]{1,0:T(8,128)(2,1)} %all-gather.2.cloned.1.call-done, bf16[256,8192]{1,0:T(8,128)(2,1)} %param.14), kind=kOutput, calls=%fused_computation.310 | convolution fusion | flops 536870912 | bytes 6422528 | tf_op jit(solution)/shard_map/dot_general | solution.py:209
  38.0 0.1 multiply_convert_fusion.1
  38.2 1.3 copy.86
  39.6 5.4 %all-to-all-start = ((bf16[4,2,1,128,256]{4,1,0,2,3:T(2,128)(2,1)}), bf16[4,2,1,128,256]{4,1,0,2,3:T(2,128)(2,1)S(1)}, u32[]{:S(2)}, u32[]{:S(2)}) async-start(bf16[4,2,1,128,256]{4,1,0,2,3:T(2,128)(2,1)} %copy.86), calls=%async_computation | async-start | bytes 1048576 | tf_op jit(solution)/shard_map/all_to_all | solution.py:75
  45.0 0.1 multiply_sine_fusion.6
  45.1 0.1 multiply_sine_fusion.8
  45.2 12.2 %all-to-all-done = bf16[4,2,1,128,256]{4,1,0,2,3:T(2,128)(2,1)S(1)} async-done(((bf16[4,2,1,128,256]{4,1,0,2,3:T(2,128)(2,1)}), bf16[4,2,1,128,256]{4,1,0,2,3:T(2,128)(2,1)S(1)}, u32[]{:S(2)}, u32[]{:S(2)}) %all-to-all-start) | async-done | bytes 524320 | tf_op jit(solution)/shard_map/all_to_all | solution.py:75
  57.4 0.1 copy.87
  57.6 0.5 fusion.33
  58.0 0.5 fusion.34
  58.5 0.5 fusion.15
  59.0 0.5 fusion.14
  59.5 0.1 pad_maximum_fusion.3
  59.6 0.9 copy.90
  60.5 5.9 %all-to-all-start.1 = ((bf16[4,2,8,16,256]{4,3,0,1,2:T(8,128)(2,1)}), bf16[4,2,8,16,256]{4,3,0,1,2:T(8,128)(2,1)S(1)}, u32[]{:S(2)}, u32[]{:S(2)}) async-start(bf16[4,2,8,16,256]{4,3,0,1,2:T(8,128)(2,1)} %copy.90), calls=%async_computation.1 | async-start | bytes 1048576 | tf_op jit(solution)/shard_map/all_to_all | solution.py:85
  66.4 2.0 fusion.5
  68.4 0.1 copy.100
  68.5 0.1 copy.99
  68.6 0.1 copy.95
  68.7 0.1 copy.98
  68.8 0.1 multiply_sine_fusion.12
  68.9 0.1 multiply_sine_fusion.11
  68.9 9.6 %all-to-all-done.1 = bf16[4,2,8,16,256]{4,3,0,1,2:T(8,128)(2,1)S(1)} async-done(((bf16[4,2,8,16,256]{4,3,0,1,2:T(8,128)(2,1)}), bf16[4,2,8,16,256]{4,3,0,1,2:T(8,128)(2,1)S(1)}, u32[]{:S(2)}, u32[]{:S(2)}) %all-to-all-start.1) | async-done | bytes 524320 | tf_op jit(solution)/shard_map/all_to_all | solution.py:85
  78.6 0.1 bitcast_convert_fusion
  78.7 1.2 fusion.61
  79.9 1.2 fusion.59
  81.1 1.2 fusion.9
  82.3 1.2 fusion.8
  83.5 0.1 multiply_subtract_fusion.1
  83.6 0.1 fusion.42
  83.7 0.1 fusion.46
  83.9 1.0 fusion.17
  85.0 1.0 fusion.16
  86.0 1.0 convolution_add_fusion
  87.0 1.1 fusion.18
  88.2 0.1 pad_maximum_fusion
  88.3 0.8 copy.101
  89.0 23.7 %all_to_all.42 = bf16[6,2,1,128,256]{4,1,2,0,3:T(2,128)(2,1)S(1)} all-to-all(bf16[6,2,1,128,256]{4,1,2,0,3:T(2,128)(2,1)S(1)} %copy.101), channel_id=1, replica_groups=mesh['ctx'=8,'tp'=4] {'ctx'}, dimensions={3} | all-to-all | bytes 1572864 | tf_op jit(solution)/shard_map/all_to_all | solution.py:75
  112.7 0.1 copy.102
  112.8 0.1 fusion.192
  112.9 0.5 fusion.25
  113.4 0.5 fusion.26
  113.9 0.6 fusion.13
  114.5 0.6 fusion.12
  115.1 0.1 pad_maximum_fusion.1
  115.2 1.1 copy.105
  116.2 5.7 %all-to-all-start.3 = ((bf16[6,2,8,16,256]{4,3,0,1,2:T(8,128)(2,1)}), bf16[6,2,8,16,256]{4,3,0,1,2:T(8,128)(2,1)S(1)}, u32[]{:S(2)}, u32[]{:S(2)}) async-start(bf16[6,2,8,16,256]{4,3,0,1,2:T(8,128)(2,1)} %copy.105), calls=%async_computation.3 | async-start | bytes 1572864 | tf_op jit(solution)/shard_map/all_to_all | solution.py:85
  121.9 17.4 %all-to-all-done.3 = bf16[6,2,8,16,256]{4,3,0,1,2:T(8,128)(2,1)S(1)} async-done(((bf16[6,2,8,16,256]{4,3,0,1,2:T(8,128)(2,1)}), bf16[6,2,8,16,256]{4,3,0,1,2:T(8,128)(2,1)S(1)}, u32[]{:S(2)}, u32[]{:S(2)}) %all-to-all-start.3) | async-done | bytes 786464 | tf_op jit(solution)/shard_map/all_to_all | solution.py:85
  139.3 0.2 fusion.191
  139.6 0.1 copy.106
  139.7 0.1 copy.107
  139.7 0.1 fusion.22
  139.9 0.5 copy-done.2
  140.4 0.8 fusion.36
  141.2 0.7 copy-done
  141.9 2.1 convolution_convert_fusion
  144.1 1.5 copy-done.1
  145.6 4.5 %fusion.197 = f32[256,8192]{1,0:T(8,128)} fusion(bf16[128,256]{1,0:T(8,128)(2,1)S(1)} %get-tuple-element.42, bf16[128,8192]{1,0:T(8,128)(2,1)S(1)} %copy-done.1), kind=kOutput, calls=%fused_computation.311 | convolution fusion | flops 536870912 | bytes 10551296 | tf_op jit(solution)/shard_map/dot_general | solution.py:226
  150.2 0.7 multiply_reduce_fusion
  151.0 29.3 %all-reduce.1 = (f32[256]{0:T(256)}, f32[16,256]{1,0:T(8,128)}, f32[16,256]{1,0:T(8,128)}) all-reduce(f32[256]{0:T(256)S(1)} %get-tuple-element.45, f32[16,256]{1,0:T(8,128)S(1)} %get-tuple-element.53, f32[16,256]{1,0:T(8,128)S(1)} %get-tuple-element.52), channel_id=1, replica_groups=mesh['ctx'=8,'tp'=4] {'ctx'}, use_global_device_ids=true, to_apply=%region_7.8 | all-reduce | flops 8448 | bytes 67584 | tf_op jit(solution)/shard_map/psum | solution.py:235
  180.3 148.6 %reduce-scatter.5.cloned.1.call-done = f32[256,1024]{1,0:T(8,128)} async-done(((f32[256,8192]{1,0:T(8,128)}), f32[256,1024]{1,0:T(8,128)}) %reduce-scatter.5.cloned.1.call-update) | async-done | bytes 1048592 | tf_op jit(solution)/shard_map/reduce_scatter | solution.py:229
  (40 shorter events, 0.7 us)
Async XLA Ops:
  7.2 26.4 %all-gather.2.cloned.1.call-start = ((), (), s32[]{:S(2)}) async-start(), calls=%async_computation.6 | async-start | bytes 2621440 | tf_op jit(solution)/shard_map/all_gather | solution.py:208
  8.8 29.1 %copy-start.4 = (bf16[128,256]{1,0:T(8,128)(2,1)S(1)}, bf16[128,256]{1,0:T(8,128)(2,1)}, u32[]{:S(2)}) copy-start(bf16[128,256]{1,0:T(8,128)(2,1)} %param.8) | copy-start | bytes 196612
  38.0 7.1 %copy-start.5 = (f32[16,256]{1,0:T(8,128)S(1)}, f32[16,256]{1,0:T(8,128)}, u32[]{:S(2)}) copy-start(f32[16,256]{1,0:T(8,128)} %param.12) | copy-start | bytes 49156
  38.0 7.1 %copy-start.6 = (f32[16,256]{1,0:T(8,128)S(1)}, f32[16,256]{1,0:T(8,128)}, u32[]{:S(2)}) copy-start(f32[16,256]{1,0:T(8,128)} %param.11) | copy-start | bytes 49156
  39.6 17.8 %all-to-all-start = ((bf16[4,2,1,128,256]{4,1,0,2,3:T(2,128)(2,1)}), bf16[4,2,1,128,256]{4,1,0,2,3:T(2,128)(2,1)S(1)}, u32[]{:S(2)}, u32[]{:S(2)}) async-start(bf16[4,2,1,128,256]{4,1,0,2,3:T(2,128)(2,1)} %copy.86), calls=%async_computation | async-start | bytes 1048576 | tf_op jit(solution)/shard_map/all_to_all | solution.py:75
  60.5 18.1 %all-to-all-start.1 = ((bf16[4,2,8,16,256]{4,3,0,1,2:T(8,128)(2,1)}), bf16[4,2,8,16,256]{4,3,0,1,2:T(8,128)(2,1)S(1)}, u32[]{:S(2)}, u32[]{:S(2)}) async-start(bf16[4,2,8,16,256]{4,3,0,1,2:T(8,128)(2,1)} %copy.90), calls=%async_computation.1 | async-start | bytes 1048576 | tf_op jit(solution)/shard_map/all_to_all | solution.py:85
  116.2 23.1 %all-to-all-start.3 = ((bf16[6,2,8,16,256]{4,3,0,1,2:T(8,128)(2,1)}), bf16[6,2,8,16,256]{4,3,0,1,2:T(8,128)(2,1)S(1)}, u32[]{:S(2)}, u32[]{:S(2)}) async-start(bf16[6,2,8,16,256]{4,3,0,1,2:T(8,128)(2,1)} %copy.105), calls=%async_computation.3 | async-start | bytes 1572864 | tf_op jit(solution)/shard_map/all_to_all | solution.py:85
  121.9 58.4 %reduce-scatter.3.cloned.1.call-start = ((), (), s32[]{:S(2)}) async-start(), calls=%async_computation.7 | async-start | bytes 2621440 | tf_op jit(solution)/shard_map/reduce_scatter | solution.py:223
  139.6 0.8 copy-start.2
  139.6 0.9 copy-start.3
  139.6 0.9 copy-start.7
  139.6 2.3 copy-start
  144.0 1.6 copy-start.1
  144.0 184.9 %reduce-scatter.5.cloned.1.call-start = ((), (), s32[]{:S(2)}) async-start(), calls=%async_computation.8 | async-start | bytes 9437184 | tf_op jit(solution)/shard_map/reduce_scatter | solution.py:229
Sparse Core Ops, SparseCore 0:
  9.6 23.9 all-gather.1
  144.2 32.2 reduce-scatter.2
  181.1 147.7 reduce-scatter.4
where the time goes:
time: 339 us; the launch traced here: 335 us
  waiting for transfers between devices  213 us (63%)
  blocking collectives  53 us (16%)
  matrix products  24 us (7%)
  starting transfers between devices  17.1 us (5%)
  between operations  14.3 us (4%)
  local copies, waits for them, and re-layouts  7.91 us (2%)
  other arithmetic  5.86 us (2%)
    reduce_scatter x1, waiting for transfers between devices, body(): lax.psum_scatter(weight_part, 'ctx', scatter_dimension=1, tiled=True)  149 us
    psum x1, blocking collectives, body(): lax.psum((skip_part, grad_res_part, grad_decay_part), 'ctx')  29.3 us
    all_to_all x2, waiting for transfers between devices, transpose_transform(): lax.all_to_all(for_sending(combined), 'ctx', split_axis=2, concat_axis=3,...  27 us
    all_gather x1, waiting for transfers between devices, body(): full_grad = lax.all_gather(out_grad, 'tp', axis=1, tiled=True)  24.7 us
    all_to_all x1, blocking collectives, transpose_transform(): lax.all_to_all(for_sending(shaped), 'ctx', split_axis=3, concat_axis=2, t...  23.7 us
    all_to_all x1, waiting for transfers between devices, transpose_transform(): lax.all_to_all(for_sending(shaped), 'ctx', split_axis=3, concat_axis=2, t...  12.2 us
    all_to_all x2, starting transfers between devices, transpose_transform(): lax.all_to_all(for_sending(combined), 'ctx', split_axis=2, concat_axis=3,...  11.6 us
  transfers between devices with their start and end apart: 6, of which 5 were waited for; matrix products, arithmetic and copies ran while one was open for 3% of the time, Pallas kernels for 0%

commit v1 on v0

--- a/solution.py
+++ b/solution.py
@@ -1,8 +1,11 @@
+import functools
 import math
 
 import jax
 import jax.numpy as jnp
 from jax import lax
+from jax.experimental import pallas as pl
+from jax.experimental.pallas import tpu as pltpu
 from jax.sharding import PartitionSpec as P
 
 PRECISE = lax.Precision.HIGHEST
@@ -195,7 +198,7 @@
     return (outcomes[0], outcomes[1], grad_res_part, grad_decay_part)
 
 
-def body(outer_gate, inner_gate, values, residues, log_decay, skip_gain, out_weight, out_grad):
+def spectral_body(outer_gate, inner_gate, values, residues, log_decay, skip_gain, out_weight, out_grad):
     ctx_size = lax.axis_size("ctx")
     device = lax.axis_index("ctx")
     levels = ctx_size.bit_length() - 1
@@ -247,6 +250,586 @@
     )
 
 
+MESH = pl.DeviceIdType.MESH
+SUB = 8
+BF16 = jnp.bfloat16
+F32 = jnp.float32
+
+
+def fused_kernel(
+    n_ctx,
+    n_tp,
+    outer_ref,
+    inner_ref,
+    value_ref,
+    tab_ref,
+    skip_ref,
+    weight_hbm,
+    grad_ref,
+    mixed_ref,
+    gouter_ref,
+    ginner_ref,
+    gvalue_ref,
+    gweight_ref,
+    gskip_ref,
+    gres_ref,
+    gdec_ref,
+    w_ref,
+    og,
+    og_t,
+    res_all,
+    st1,
+    st2,
+    d_cross,
+    d_own,
+    sib_out,
+    sib_in,
+    x_out,
+    x_in,
+    u_ref,
+    y_ref,
+    gg_ref,
+    gc_ref,
+    turn_ref,
+    u_sub,
+    gc_sub,
+    rows,
+    pre,
+    pre2,
+    w_sem,
+    a_send,
+    a_recv,
+    t_send,
+    t_recv,
+    f_send,
+    f_recv,
+    e_send,
+    e_recv,
+    r_send,
+    r_recv,
+    g_send,
+    g_recv,
+    m_send,
+    m_recv,
+):
+    c = lax.axis_index("ctx")
+    t = lax.axis_index("tp")
+    core = t % 2
+    sib = t + 1 - 2 * core
+    far = (t + 2) % n_tp
+    far_sib = (sib + 2) % n_tp
+    base = t - core
+    n_rows, feats = grad_ref.shape
+    chans = outer_ref.shape[1]
+    modes = tab_ref.shape[0] // 8
+    steps = n_rows // SUB
+    block = feats * n_tp // n_ctx
+    half = block // 2
+    per = n_ctx // n_tp
+
+    def remote(src, dst, send, recv, ctx_id, tp_id):
+        return pltpu.make_async_remote_copy(
+            src_ref=src,
+            dst_ref=dst,
+            send_sem=send,
+            recv_sem=recv,
+            device_id=(ctx_id, tp_id),
+            device_id_type=MESH,
+        )
+
+    w_copy = pltpu.make_async_copy(weight_hbm, w_ref, w_sem)
+    w_copy.start()
+
+    barrier = pltpu.get_barrier_semaphore()
+
+    def greet(d, carry):
+        peer = (c + d) % n_ctx
+        for h in range(2):
+            pl.semaphore_signal(barrier, inc=1, device_id=(peer, base + h), device_id_type=MESH)
+        return carry
+
+    lax.fori_loop(1, n_ctx, greet, 0)
+    pl.semaphore_signal(barrier, inc=1, device_id=(c, sib), device_id_type=MESH)
+    pl.semaphore_signal(barrier, inc=1, device_id=(c, far), device_id_type=MESH)
+
+    u_ref[...] = inner_ref[...].astype(F32) * value_ref[...].astype(F32)
+
+    def table(which, n):
+        return tab_ref[pl.ds(which * modes + n, 1), :]
+
+    lanes = turn_ref.shape[2]
+
+    def spread(value, ref):
+        for k in range(chans // lanes):
+            turn_ref[k] = value[:, k * lanes : (k + 1) * lanes]
+        for i in range(steps):
+            for k in range(chans // lanes):
+                ref[i, :, k * lanes : (k + 1) * lanes] = turn_ref[k, pl.ds(i, SUB, stride=steps), :]
+
+    def gathered(parts):
+        for i in range(steps):
+            for k in range(chans // lanes):
+                turn_ref[k, pl.ds(i, SUB, stride=steps), :] = parts[i][:, k * lanes : (k + 1) * lanes]
+        return jnp.concatenate([turn_ref[k] for k in range(chans // lanes)], axis=1)
+
+    place = lax.broadcasted_iota(jnp.int32, (SUB, chans), 0)
+
+    def down(x, k):
+        return jnp.where(place >= k, pltpu.roll(x, k, 0), 0.0)
+
+    def up(x, k):
+        return jnp.where(place < SUB - k, pltpu.roll(x, SUB - k, 0), 0.0)
+
+    spread(u_ref[...], u_sub)
+
+    def first_states(n, carry):
+        a = jnp.broadcast_to(table(0, n), (SUB, chans))
+        q = jnp.broadcast_to(table(1, n), (SUB, chans))
+        x = jnp.zeros((SUB, chans), F32)
+        xp = jnp.zeros((SUB, chans), F32)
+        for i in range(steps):
+            xp = a * (xp + x)
+            x = a * x + u_sub[i]
+        k = 1
+        while k < SUB:
+            xs = down(x, k)
+            xp = xp + q * (down(xp, k) + (1.0 * k * steps) * xs)
+            x = x + q * xs
+            q = q * q
+            k *= 2
+        pre[n] = down(x, 1)
+        pre2[n] = down(xp, 1)
+        rows[pl.ds(n, 1), :] = x[SUB - 1 :]
+        rows[pl.ds(modes + n, 1), :] = xp[SUB - 1 :]
+        return carry
+
+    pl.semaphore_wait(barrier, 2 * n_ctx)
+
+    pieces = per
+    width = feats // pieces
+    og[t] = grad_ref[...]
+
+    def block_copies(b, slot, dst_tp):
+        return [
+            remote(
+                og.at[b, :, pl.ds(p * width, width)],
+                og.at[b, :, pl.ds(p * width, width)],
+                a_send.at[slot, p],
+                a_recv.at[slot, p],
+                c,
+                dst_tp,
+            )
+            for p in range(pieces)
+        ]
+
+    def turned(b, slot, j, h):
+        return remote(
+            og.at[b, :, pl.ds(j * block + h * half, half)],
+            og_t.at[h, c],
+            t_send.at[slot, j, h],
+            t_recv.at[c],
+            per * b + j,
+            base + h,
+        )
+
+    def start_turned(b, slot, j):
+        @pl.when(per * b + j != c)
+        def _():
+            for h in range(2):
+                turned(b, slot, j, h).start()
+
+    to_far = block_copies(t, 0, far)
+    to_sib = block_copies(t, 1, sib)
+    for cp in to_far:
+        cp.start()
+    for cp in to_sib:
+        cp.start()
+
+    lax.fori_loop(0, modes, first_states, 0)
+    st1[c] = rows[: 2 * modes, :].astype(BF16)
+
+    def e_copy(d):
+        return remote(
+            st1.at[c], st1.at[c], e_send.at[d], e_recv.at[d], (c + d) % n_ctx, t
+        )
+
+    def each_peer(action):
+        def step(d, carry):
+            action(d)
+            return carry
+
+        lax.fori_loop(1, n_ctx, step, 0)
+
+    each_peer(lambda d: e_copy(d).start())
+    for j in range(per):
+        start_turned(t, 0, j)
+
+    def e_wait(d):
+        slot = (c + n_ctx - d) % n_ctx
+        remote(st1.at[slot], st1.at[slot], e_send.at[d], e_recv.at[d], c, t).wait_recv()
+
+    each_peer(e_wait)
+
+    q_dev = tab_ref[2 * modes : 3 * modes, :]
+
+    def chain(k, carry):
+        x, xp = carry
+        block_state = st1[k].astype(F32)
+        keep = k < c
+        xp_new = q_dev * (xp + (1.0 * n_rows) * x) + block_state[modes:]
+        x_new = q_dev * x + block_state[:modes]
+        return jnp.where(keep, x_new, x), jnp.where(keep, xp_new, xp)
+
+    zero = jnp.zeros((modes, chans), F32)
+    x_in_state, xp_in_state = lax.fori_loop(0, n_ctx, chain, (zero, zero))
+    rows[:modes, :] = x_in_state
+    rows[modes : 2 * modes, :] = xp_in_state
+    offset = (place * steps).astype(F32)
+
+    def second(n, carry):
+        a = jnp.broadcast_to(table(0, n), (SUB, chans))
+        gain = jnp.broadcast_to(table(3, n), (SUB, chans))
+        fade = jnp.exp(-offset * table(4, n))
+        x0 = rows[pl.ds(n, 1), :]
+        xp0 = rows[pl.ds(modes + n, 1), :]
+        x = pre[n] + fade * x0
+        xp = pre2[n] + fade * (xp0 + offset * x0)
+        pre[n] = x
+        pre2[n] = xp
+        out = []
+        for i in range(steps):
+            x = a * x + u_sub[i]
+            out.append(carry[i] + gain * x)
+        return tuple(out)
+
+    ys = lax.fori_loop(
+        0, modes, second, tuple(jnp.zeros((SUB, chans), F32) for _ in range(steps))
+    )
+    y_ref[...] = gathered(ys) + skip_ref[...] * u_ref[...]
+
+    res_all[c] = (outer_ref[...].astype(F32) * y_ref[...]).astype(BF16)
+
+    def r_copy(d):
+        return remote(
+            res_all.at[c], res_all.at[c], r_send.at[d], r_recv.at[d], (c + d) % n_ctx, t
+        )
+
+    each_peer(lambda d: r_copy(d).start())
+
+    w_copy.wait()
+    tile = min(512, feats)
+
+    def project(dest, sink):
+        def step(k, carry):
+            col = pl.multiple_of(k * tile, tile)
+            part = jnp.dot(
+                res_all[c],
+                w_ref[:, pl.ds(pl.multiple_of(dest * feats + col, tile), tile)],
+                preferred_element_type=F32,
+            )
+            sink[:, pl.ds(col, tile)] = part.astype(sink.dtype)
+            return carry
+
+        lax.fori_loop(0, feats // tile, step, 0)
+
+    m_sib = [
+        remote(sib_out.at[k], sib_in.at[k], m_send.at[k], m_recv.at[k], c, sib) for k in range(2)
+    ]
+    m_far = remote(x_out, x_in, m_send.at[2], m_recv.at[2], c, far)
+
+    project(far_sib, sib_out.at[0])
+    m_sib[0].start()
+    project(far, d_cross)
+
+    far_in = block_copies(far, 0, far)
+    fwd = block_copies(far, 2, sib)
+    for p in range(pieces):
+        far_in[p].wait_recv()
+        fwd[p].start()
+        start_turned(far, 1, p)
+
+    m_sib[0].wait_recv()
+    x_out[...] = (d_cross[...] + sib_in[0].astype(F32)).astype(BF16)
+    m_far.start()
+
+    project(sib, sib_out.at[1])
+    m_sib[1].start()
+    project(t, d_own)
+
+    for p in range(pieces):
+        block_copies(sib, 1, sib)[p].wait_recv()
+    for p in range(pieces):
+        block_copies(far_sib, 2, sib)[p].wait_recv()
+
+    gg_ref[...] = jnp.zeros_like(gg_ref)
+
+    def back_project(b, carry):
+        for k in range(feats // tile):
+            gg_ref[...] += lax.dot_general(
+                og[b, :, pl.ds(k * tile, tile)],
+                w_ref[:, pl.ds(pl.multiple_of(b * feats + k * tile, tile), tile)],
+                (((1,), (1,)), ((), ())),
+                preferred_element_type=F32,
+            )
+        return carry
+
+    lax.fori_loop(0, n_tp, back_project, 0)
+    gc_ref[...] = gg_ref[...] * outer_ref[...].astype(F32)
+    gouter_ref[...] = (gg_ref[...] * y_ref[...]).astype(BF16)
+
+    spread(gc_ref[...], gc_sub)
+
+    def third(n, carry):
+        a = jnp.broadcast_to(table(0, n), (SUB, chans))
+        q = jnp.broadcast_to(table(1, n), (SUB, chans))
+        x = pre[n]
+        xp = pre2[n]
+        sum_a = jnp.zeros((SUB, chans), F32)
+        sum_b = jnp.zeros((SUB, chans), F32)
+        w = jnp.zeros((SUB, chans), F32)
+        for i in range(steps):
+            g = gc_sub[i]
+            xp = a * (xp + x)
+            x = a * x + u_sub[i]
+            sum_a = sum_a + g * x
+            sum_b = sum_b + g * xp
+            w = a * w + gc_sub[steps - 1 - i]
+        k = 1
+        while k < SUB:
+            w = w + q * up(w, k)
+            q = q * q
+            k *= 2
+        pre[n] = up(w, 1)
+        rows[pl.ds(n, 1), :] = w[:1]
+        rows[pl.ds(modes + n, 1), :] = jnp.sum(sum_a, axis=0, keepdims=True)
+        rows[pl.ds(2 * modes + n, 1), :] = jnp.sum(sum_b, axis=0, keepdims=True)
+        return carry
+
+    lax.fori_loop(0, modes, third, 0)
+    rows[3 * modes :, :] = jnp.broadcast_to(
+        jnp.sum(gc_ref[...] * u_ref[...], axis=0, keepdims=True), (modes, chans)
+    )
+    st2[c] = rows[...].astype(BF16)
+
+    def g_copy(d):
+        return remote(
+            st2.at[c], st2.at[c], g_send.at[d], g_recv.at[d], (c + d) % n_ctx, t
+        )
+
+    each_peer(lambda d: g_copy(d).start())
+
+    m_sib[1].wait_recv()
+    d_own[...] += sib_in[1].astype(F32)
+    m_far.wait_recv()
+    mixed_ref[...] = (d_own[...] + x_in[...].astype(F32)).astype(BF16)
+
+    def g_wait(d):
+        slot = (c + n_ctx - d) % n_ctx
+        remote(st2.at[slot], st2.at[slot], g_send.at[d], g_recv.at[d], c, t).wait_recv()
+
+    each_peer(g_wait)
+
+    def chain_back(k, carry):
+        w, total = carry
+        dev = n_ctx - 1 - k
+        state = st2[dev].astype(F32)
+        return (
+            jnp.where(dev > c, q_dev * w + state[:modes], w),
+            total + state[modes:],
+        )
+
+    w_state, total = lax.fori_loop(
+        0, n_ctx, chain_back, (zero, jnp.zeros((3 * modes, chans), F32))
+    )
+    rows[:modes, :] = w_state
+    fac = tab_ref[5 * modes : 6 * modes, :]
+    gres_ref[...] = fac * total[:modes]
+    gdec_ref[...] = (
+        tab_ref[6 * modes : 7 * modes, :] * total[:modes]
+        - tab_ref[7 * modes :, :] * total[modes : 2 * modes]
+    )
+    gskip_ref[...] = total[2 * modes : 2 * modes + 1]
+
+    back_offset = ((SUB - 1 - place) * steps).astype(F32)
+
+    def fourth(n, carry):
+        a = jnp.broadcast_to(table(0, n), (SUB, chans))
+        gain = jnp.broadcast_to(table(3, n), (SUB, chans))
+        w = pre[n] + jnp.exp(-back_offset * table(4, n)) * rows[pl.ds(n, 1), :]
+        out = []
+        for i in range(steps):
+            w = a * w + gc_sub[steps - 1 - i]
+            out.append(carry[i] + gain * w)
+        return tuple(out)
+
+    ws = lax.fori_loop(
+        0, modes, fourth, tuple(jnp.zeros((SUB, chans), F32) for _ in range(steps))
+    )
+    y_ref[...] = gathered(ws[::-1]) + skip_ref[...] * gc_ref[...]
+    ginner_ref[...] = (y_ref[...] * value_ref[...].astype(F32)).astype(BF16)
+    gvalue_ref[...] = (y_ref[...] * inner_ref[...].astype(F32)).astype(BF16)
+
+    own_b = c // per
+    own_j = c % per
+    for h in range(2):
+        og_t[h, c] = og[own_b, :, pl.ds(pl.multiple_of(own_j * block + h * half, half), half)]
+
+    def f_copy(slot, h):
+        return remote(
+            og_t.at[h, slot], og_t.at[h, slot], f_send.at[slot], f_recv.at[slot], c, sib
+        )
+
+    def pass_on(d):
+        slot = (c + n_ctx - d) % n_ctx
+        remote(
+            og_t.at[core, slot], og_t.at[core, slot], t_send.at[0, 0, 0], t_recv.at[slot], c, t
+        ).wait_recv()
+        f_copy(slot, core).start()
+
+    each_peer(pass_on)
+
+    def r_wait(d):
+        slot = (c + n_ctx - d) % n_ctx
+        remote(
+            res_all.at[slot], res_all.at[slot], r_send.at[d], r_recv.at[d], c, t
+        ).wait_recv()
+
+    each_peer(r_wait)
+
+    def weigh(h):
+        left = res_all[...].reshape(n_ctx * n_rows, chans)
+        right = og_t[h].reshape(n_ctx * n_rows, half)
+        gweight_ref[:, pl.ds(pl.multiple_of(h * half, half), half)] = lax.dot_general(
+            left, right, (((0,), (0,)), ((), ())), preferred_element_type=F32
+        )
+
+    weigh(core)
+
+    def f_wait(d):
+        slot = (c + n_ctx - d) % n_ctx
+        f_copy(slot, 1 - core).wait_recv()
+
+    each_peer(f_wait)
+    weigh(1 - core)
+
+    for cp in to_far + to_sib + fwd:
+        cp.wait_send()
+    for slot, b in enumerate((t, far)):
+        for j in range(per):
+
+            @pl.when(per * b + j != c)
+            def _():
+                for h in range(2):
+                    turned(b, slot, j, h).wait_send()
+
+    def sent(d):
+        slot = (c + n_ctx - d) % n_ctx
+        f_copy(slot, core).wait_send()
+        e_copy(d).wait_send()
+        r_copy(d).wait_send()
+        g_copy(d).wait_send()
+
+    each_peer(sent)
+    for cp in m_sib + [m_far]:
+        cp.wait_send()
+
+
+def fused_body(
+    n_ctx, n_tp, outer_gate, inner_gate, values, residues, log_decay, skip_gain, out_weight, out_grad
+):
+    n_rows, chans = outer_gate.shape
+    feats = out_grad.shape[1]
+    modes = residues.shape[0]
+    steps = n_rows // SUB
+    block = feats * n_tp // n_ctx
+    per = n_ctx // n_tp
+    rate = jnp.exp(log_decay)
+    fac = jnp.sqrt(-jnp.expm1(-2.0 * rate))
+    tables = jnp.concatenate(
+        [
+            jnp.exp(-rate),
+            jnp.exp(-rate * steps),
+            jnp.exp(-rate * n_rows),
+            residues * fac,
+            rate,
+            fac,
+            rate * residues * jnp.exp(-2.0 * rate) / fac,
+            rate * residues * fac,
+        ],
+        axis=0,
+    )
+    vmem = pl.BlockSpec(memory_space=pltpu.VMEM)
+    dma = pltpu.SemaphoreType.DMA
+    outs = pl.pallas_call(
+        functools.partial(fused_kernel, n_ctx, n_tp),
+        out_shape=(
+            jax.ShapeDtypeStruct((n_rows, feats), BF16),
+            jax.ShapeDtypeStruct((n_rows, chans), BF16),
+            jax.ShapeDtypeStruct((n_rows, chans), BF16),
+            jax.ShapeDtypeStruct((n_rows, chans), BF16),
+            jax.ShapeDtypeStruct((chans, block), F32),
+            jax.ShapeDtypeStruct((1, chans), F32),
+            jax.ShapeDtypeStruct((modes, chans), F32),
+            jax.ShapeDtypeStruct((modes, chans), F32),
+        ),
+        in_specs=[vmem] * 5 + [pl.BlockSpec(memory_space=pl.ANY), vmem],
+        out_specs=(vmem,) * 8,
+        scratch_shapes=[
+            pltpu.VMEM(out_weight.shape, BF16),
+            pltpu.VMEM((n_tp, n_rows, feats), BF16),
+            pltpu.VMEM((2, n_ctx, n_rows, block // 2), BF16),
+            pltpu.VMEM((n_ctx, n_rows, chans), BF16),
+            pltpu.VMEM((n_ctx, 2 * modes, chans), BF16),
+            pltpu.VMEM((n_ctx, 4 * modes, chans), BF16),
+            pltpu.VMEM((n_rows, feats), F32),
+            pltpu.VMEM((n_rows, feats), F32),
+            pltpu.VMEM((2, n_rows, feats), BF16),
+            pltpu.VMEM((2, n_rows, feats), BF16),
+            pltpu.VMEM((n_rows, feats), BF16),
+            pltpu.VMEM((n_rows, feats), BF16),
+            pltpu.VMEM((n_rows, chans), F32),
+            pltpu.VMEM((n_rows, chans), F32),
+            pltpu.VMEM((n_rows, chans), F32),
+            pltpu.VMEM((n_rows, chans), F32),
+            pltpu.VMEM((chans // 128, n_rows, 128), F32),
+            pltpu.VMEM((steps, SUB, chans), F32),
+            pltpu.VMEM((steps, SUB, chans), F32),
+            pltpu.VMEM((4 * modes, chans), F32),
+            pltpu.VMEM((modes, SUB, chans), F32),
+            pltpu.VMEM((modes, SUB, chans), F32),
+            dma,
+            dma((3, per)),
+            dma((3, per)),
+            dma((2, per, 2)),
+            dma((n_ctx,)),
+            dma((n_ctx,)),
+            dma((n_ctx,)),
+            dma((n_ctx,)),
+            dma((n_ctx,)),
+            dma((n_ctx,)),
+            dma((n_ctx,)),
+            dma((n_ctx,)),
+            dma((n_ctx,)),
+            dma((3,)),
+            dma((3,)),
+        ],
+        compiler_params=pltpu.CompilerParams(
+            collective_id=0, has_side_effects=True, vmem_limit_bytes=48 * 2**20
+        ),
+    )(outer_gate, inner_gate, values, tables, skip_gain[None, :], out_weight, out_grad)
+    return outs[:5] + (outs[5][0],) + outs[6:]
+
+
+def body(n_ctx, n_tp, *arrays):
+    n_rows = arrays[0].shape[0]
+    feats = arrays[-1].shape[1]
+    modes = arrays[3].shape[0]
+    pairs = n_tp == 4 and n_ctx % n_tp == 0 and (feats * n_tp // n_ctx) % 256 == 0
+    if pairs and n_rows % 16 == 0 and modes % 16 == 0:
+        return fused_body(n_ctx, n_tp, *arrays)
+    return spectral_body(*arrays)
+
+
 def solution(mesh):
     placed = (
         P("ctx", "tp"),
@@ -259,7 +842,7 @@
         P("ctx", "tp"),
     )
     return jax.shard_map(
-        body,
+        functools.partial(body, mesh.shape["ctx"], mesh.shape["tp"]),
         mesh=mesh,
         in_specs=placed,
         out_specs=(

time: 339 us -> 82.4 us (0.24)
  waiting for transfers between devices: 213 us -> 0 us
  Pallas kernels: 0 us -> 64.9 us
  blocking collectives: 53 us -> 0 us
  matrix products: 24 us -> 0 us
  starting transfers between devices: 17.1 us -> 0 us
  between operations: 14.3 us -> 0.69 us
    reduce_scatter x2 -> x0, waiting for transfers between devices: 149 us -> none  [the longest x1 149 us: body(): lax.psum_scatter(weight_part, 'ctx', scatter_dimension=1, tiled=True)]
    pallas_call x0 -> x1, Pallas kernels: none -> 64.9 us  [fused_body(): pl.pallas_call(functools.partial(fused_kernel, n_ctx, n_tp), out_shape=(j...]
    all_to_all x3 -> x0, waiting for transfers between devices: 39.2 us -> none  [the longest x2 27 us: transpose_transform(): lax.all_to_all(for_sending(combined), 'ctx', split_axis=2, concat_axis=3,...]
    psum x1 -> x0, blocking collectives: 29.3 us -> none  [body(): lax.psum((skip_part, grad_res_part, grad_decay_part), 'ctx')]
    all_gather x1 -> x0, waiting for transfers between devices: 24.7 us -> none  [body(): full_grad = lax.all_gather(out_grad, 'tp', axis=1, tiled=True)]
    dot_general x19 -> x0, matrix products: 24 us -> none  [the longest x1 4.51 us: body(): lax.dot_general(result, full_grad, (((0,), (0,)), ((), ())), preferred_el...]
    all_to_all x1 -> x0, blocking collectives: 23.7 us -> none  [transpose_transform(): lax.all_to_all(for_sending(shaped), 'ctx', split_axis=3, concat_axis=2, t...]
    all_to_all x3 -> x0, starting transfers between devices: 17 us -> none  [the longest x2 11.6 us: transpose_transform(): lax.all_to_all(for_sending(combined), 'ctx', split_axis=2, concat_axis=3,...]
  transfers between devices with their start and end apart: 6 -> 0, of which waited for: 5 -> 0; matrix products, arithmetic and copies ran while one was open for 3% -> 0% of each run, Pallas kernels for 0% -> 0%
where the time goes in v1:
time: 82.4 us; the launch traced here: 81.2 us
  Pallas kernels  64.9 us (79%)
  local copies, waits for them, and re-layouts  10.4 us (13%)
  other arithmetic  5.23 us (6%)
    pallas_call x1, Pallas kernels, fused_body(): pl.pallas_call(functools.partial(fused_kernel, n_ctx, n_tp), out_shape=(j...  64.9 us
    unnamed x19, local copies, waits for them, and re-layouts  10.4 us
    unnamed x6, other arithmetic  4.47 us

profile of v1, /device:TPU:25, one launch (start us, length us, event | category | flops | bytes accessed | tf_op | source)
XLA Modules:
  0.0 81.2 jit_solution(11874440957343816439)
XLA Ops:
  0.6 0.7 constant_dynamic-update-slice_fusion.7
  1.4 0.7 constant_dynamic-update-slice_fusion.6
  2.1 0.7 constant_dynamic-update-slice_fusion.5
  2.8 0.8 constant_dynamic-update-slice_fusion.4
  3.6 0.7 constant_dynamic-update-slice_fusion.3
  4.3 0.7 constant_dynamic-update-slice_fusion.2
  5.1 0.8 constant_dynamic-update-slice_fusion.1
  5.9 0.8 constant_dynamic-update-slice_fusion.tab_ref
  6.6 0.0 copy-start
  6.6 1.0 %copy-done = bf16[128,2048]{1,0:T(8,128)(2,1)S(1)} copy-done((bf16[128,2048]{1,0:T(8,128)(2,1)S(1)}, bf16[128,2048]{1,0:T(8,128)(2,1)}, u32[]{:S(2)}) %copy-start) | copy-done | bytes 524312
  7.7 0.0 copy-start.1
  7.7 0.8 %copy-done.1 = bf16[128,256]{1,0:T(8,128)(2,1)S(1)} copy-done((bf16[128,256]{1,0:T(8,128)(2,1)S(1)}, bf16[128,256]{1,0:T(8,128)(2,1)}, u32[]{:S(2)}) %copy-start.1) | copy-done | bytes 65560
  8.5 0.0 copy-start.2
  8.5 0.8 %copy-done.2 = bf16[128,256]{1,0:T(8,128)(2,1)S(1)} copy-done((bf16[128,256]{1,0:T(8,128)(2,1)S(1)}, bf16[128,256]{1,0:T(8,128)(2,1)}, u32[]{:S(2)}) %copy-start.2) | copy-done | bytes 65560
  9.4 0.0 copy-start.3
  9.4 0.8 %copy-done.3 = bf16[128,256]{1,0:T(8,128)(2,1)S(1)} copy-done((bf16[128,256]{1,0:T(8,128)(2,1)S(1)}, bf16[128,256]{1,0:T(8,128)(2,1)}, u32[]{:S(2)}) %copy-start.3) | copy-done | bytes 65560
  10.2 0.0 copy-start.4
  10.2 0.7 copy-done.4
  10.9 64.9 %shard_map.143 = (bf16[128,2048]{1,0:T(8,128)(2,1)S(1)}, bf16[128,256]{1,0:T(8,128)(2,1)S(1)}, bf16[128,256]{1,0:T(8,128)(2,1)S(1)}, bf16[128,256]{1,0:T(8,128)(...) custom-call(bf16[128,256]{1,0:T(8,128)(2,1)S(1)} %copy-done.1, ...), custom_call_target="tpu_custom_call" | custom-call | tf_op jit(solution)/shard_map/pallas_call | solution.py:763
  75.8 0.8 copy.31
  76.6 0.6 copy.32
  77.2 0.6 copy.33
  77.8 0.6 copy.34
  78.5 1.0 %copy.35 = f32[256,1024]{1,0:T(8,128)} copy(f32[256,1024]{1,0:T(8,128)S(1)} %get-tuple-element.36) | data formatting | bytes 2097152
  79.4 0.6 copy.36
  80.0 0.6 copy.37
  80.6 0.6 copy.38
Async XLA Ops:
  6.6 1.0 %copy-start = (bf16[128,2048]{1,0:T(8,128)(2,1)S(1)}, bf16[128,2048]{1,0:T(8,128)(2,1)}, u32[]{:S(2)}) copy-start(bf16[128,2048]{1,0:T(8,128)(2,1)} %grad_ref.1) | copy-start | bytes 1572868
  7.7 0.8 %copy-start.1 = (bf16[128,256]{1,0:T(8,128)(2,1)S(1)}, bf16[128,256]{1,0:T(8,128)(2,1)}, u32[]{:S(2)}) copy-start(bf16[128,256]{1,0:T(8,128)(2,1)} %outer_ref.1) | copy-start | bytes 196612
  8.5 0.8 %copy-start.2 = (bf16[128,256]{1,0:T(8,128)(2,1)S(1)}, bf16[128,256]{1,0:T(8,128)(2,1)}, u32[]{:S(2)}) copy-start(bf16[128,256]{1,0:T(8,128)(2,1)} %inner_ref.1) | copy-start | bytes 196612
  9.4 0.8 %copy-start.3 = (bf16[128,256]{1,0:T(8,128)(2,1)S(1)}, bf16[128,256]{1,0:T(8,128)(2,1)}, u32[]{:S(2)}) copy-start(bf16[128,256]{1,0:T(8,128)(2,1)} %value_ref.1) | copy-start | bytes 196612
  10.2 0.7 copy-start.4

commit v2 on v1

--- a/solution.py
+++ b/solution.py
@@ -259,13 +259,14 @@
 def fused_kernel(
     n_ctx,
     n_tp,
-    outer_ref,
-    inner_ref,
-    value_ref,
-    tab_ref,
-    skip_ref,
+    outer_hbm,
+    inner_hbm,
+    value_hbm,
+    res_hbm,
+    dec_hbm,
+    skip_hbm,
     weight_hbm,
-    grad_ref,
+    grad_hbm,
     mixed_ref,
     gouter_ref,
     ginner_ref,
@@ -274,6 +275,12 @@
     gskip_ref,
     gres_ref,
     gdec_ref,
+    outer_ref,
+    inner_ref,
+    value_ref,
+    modal_ref,
+    skip_ref,
+    tab_ref,
     w_ref,
     og,
     og_t,
@@ -296,6 +303,7 @@
     rows,
     pre,
     pre2,
+    in_sem,
     w_sem,
     a_send,
     a_recv,
@@ -319,12 +327,12 @@
     far = (t + 2) % n_tp
     far_sib = (sib + 2) % n_tp
     base = t - core
-    n_rows, feats = grad_ref.shape
+    n_rows, feats = grad_hbm.shape
     chans = outer_ref.shape[1]
-    modes = tab_ref.shape[0] // 8
+    modes = modal_ref.shape[1]
     steps = n_rows // SUB
     block = feats * n_tp // n_ctx
-    half = block // 2
+    share = block // n_tp
     per = n_ctx // n_tp
 
     def remote(src, dst, send, recv, ctx_id, tp_id):
@@ -338,7 +346,22 @@
         )
 
     w_copy = pltpu.make_async_copy(weight_hbm, w_ref, w_sem)
-    w_copy.start()
+    loads = [
+        pltpu.make_async_copy(src, dst, in_sem.at[k])
+        for k, (src, dst) in enumerate(
+            (
+                (grad_hbm, og.at[t]),
+                (dec_hbm, modal_ref.at[0]),
+                (res_hbm, modal_ref.at[1]),
+                (inner_hbm, inner_ref),
+                (value_hbm, value_ref),
+                (outer_hbm, outer_ref),
+                (skip_hbm, skip_ref),
+            )
+        )
+    ]
+    for load in loads:
+        load.start()
 
     barrier = pltpu.get_barrier_semaphore()
 
@@ -351,6 +374,32 @@
     lax.fori_loop(1, n_ctx, greet, 0)
     pl.semaphore_signal(barrier, inc=1, device_id=(c, sib), device_id_type=MESH)
     pl.semaphore_signal(barrier, inc=1, device_id=(c, far), device_id_type=MESH)
+
+    for load in loads[1:]:
+        load.wait()
+    w_copy.start()
+    rate = jnp.exp(modal_ref[0])
+    twice = 2.0 * rate
+    series = twice * (
+        1.0
+        - twice / 2.0
+        * (1.0 - twice / 3.0 * (1.0 - twice / 4.0 * (1.0 - twice / 5.0 * (1.0 - twice / 6.0 * (1.0 - twice / 7.0)))))
+    )
+    fac = jnp.sqrt(jnp.where(twice < 0.3, series, 1.0 - jnp.exp(-twice)))
+    weighted = modal_ref[1] * fac
+    for k, part in enumerate(
+        (
+            jnp.exp(-rate),
+            jnp.exp(-rate * steps),
+            jnp.exp(-rate * n_rows),
+            weighted,
+            rate,
+            fac,
+            rate * modal_ref[1] * jnp.exp(-twice) / fac,
+            rate * weighted,
+        )
+    ):
+        tab_ref[k * modes : (k + 1) * modes, :] = part
 
     u_ref[...] = inner_ref[...].astype(F32) * value_ref[...].astype(F32)
 
@@ -407,7 +456,7 @@
 
     pieces = per
     width = feats // pieces
-    og[t] = grad_ref[...]
+    loads[0].wait()
 
     def block_copies(b, slot, dst_tp):
         return [
@@ -424,8 +473,8 @@
 
     def turned(b, slot, j, h):
         return remote(
-            og.at[b, :, pl.ds(j * block + h * half, half)],
-            og_t.at[h, c],
+            og.at[b, :, pl.ds(pl.multiple_of(j * block + (base + h) * share, share), share)],
+            og_t.at[base + h, c],
             t_send.at[slot, j, h],
             t_recv.at[c],
             per * b + j,
@@ -618,10 +667,59 @@
 
     each_peer(lambda d: g_copy(d).start())
 
+    own_b = c // per
+    own_j = c % per
+    for h in range(n_tp):
+        og_t[h, c] = og[own_b, :, pl.ds(pl.multiple_of(own_j * block + h * share, share), share)]
+
+    def f_copy(way, slot, h, dest):
+        return remote(
+            og_t.at[h, slot],
+            og_t.at[h, slot],
+            f_send.at[way, slot],
+            f_recv.at[way, slot],
+            c,
+            dest,
+        )
+
+    def pass_on(d):
+        slot = (c + n_ctx - d) % n_ctx
+        remote(
+            og_t.at[t, slot], og_t.at[t, slot], t_send.at[0, 0, 0], t_recv.at[slot], c, t
+        ).wait_recv()
+        f_copy(0, slot, t, far).start()
+        f_copy(1, slot, t, sib).start()
+
+    each_peer(pass_on)
+
     m_sib[1].wait_recv()
     d_own[...] += sib_in[1].astype(F32)
     m_far.wait_recv()
     mixed_ref[...] = (d_own[...] + x_in[...].astype(F32)).astype(BF16)
+
+    def r_wait(d):
+        slot = (c + n_ctx - d) % n_ctx
+        remote(
+            res_all.at[slot], res_all.at[slot], r_send.at[d], r_recv.at[d], c, t
+        ).wait_recv()
+
+    each_peer(r_wait)
+
+    def weigh(h):
+        left = res_all[...].reshape(n_ctx * n_rows, chans)
+        right = og_t[h].reshape(n_ctx * n_rows, share)
+        gweight_ref[:, pl.ds(pl.multiple_of(h * share, share), share)] = lax.dot_general(
+            left, right, (((0,), (0,)), ((), ())), preferred_element_type=F32
+        )
+
+    weigh(t)
+
+    def pass_far(d):
+        slot = (c + n_ctx - d) % n_ctx
+        f_copy(0, slot, far, far).wait_recv()
+        f_copy(2, slot, far, sib).start()
+
+    each_peer(pass_far)
 
     def g_wait(d):
         slot = (c + n_ctx - d) % n_ctx
@@ -642,8 +740,7 @@
         0, n_ctx, chain_back, (zero, jnp.zeros((3 * modes, chans), F32))
     )
     rows[:modes, :] = w_state
-    fac = tab_ref[5 * modes : 6 * modes, :]
-    gres_ref[...] = fac * total[:modes]
+    gres_ref[...] = tab_ref[5 * modes : 6 * modes, :] * total[:modes]
     gdec_ref[...] = (
         tab_ref[6 * modes : 7 * modes, :] * total[:modes]
         - tab_ref[7 * modes :, :] * total[modes : 2 * modes]
@@ -669,48 +766,19 @@
     ginner_ref[...] = (y_ref[...] * value_ref[...].astype(F32)).astype(BF16)
     gvalue_ref[...] = (y_ref[...] * inner_ref[...].astype(F32)).astype(BF16)
 
-    own_b = c // per
-    own_j = c % per
-    for h in range(2):
-        og_t[h, c] = og[own_b, :, pl.ds(pl.multiple_of(own_j * block + h * half, half), half)]
-
-    def f_copy(slot, h):
-        return remote(
-            og_t.at[h, slot], og_t.at[h, slot], f_send.at[slot], f_recv.at[slot], c, sib
-        )
-
-    def pass_on(d):
-        slot = (c + n_ctx - d) % n_ctx
-        remote(
-            og_t.at[core, slot], og_t.at[core, slot], t_send.at[0, 0, 0], t_recv.at[slot], c, t
-        ).wait_recv()
-        f_copy(slot, core).start()
-
-    each_peer(pass_on)
-
-    def r_wait(d):
-        slot = (c + n_ctx - d) % n_ctx
-        remote(
-            res_all.at[slot], res_all.at[slot], r_send.at[d], r_recv.at[d], c, t
-        ).wait_recv()
-
-    each_peer(r_wait)
-
-    def weigh(h):
-        left = res_all[...].reshape(n_ctx * n_rows, chans)
-        right = og_t[h].reshape(n_ctx * n_rows, half)
-        gweight_ref[:, pl.ds(pl.multiple_of(h * half, half), half)] = lax.dot_general(
-            left, right, (((0,), (0,)), ((), ())), preferred_element_type=F32
-        )
-
-    weigh(core)
-
-    def f_wait(d):
-        slot = (c + n_ctx - d) % n_ctx
-        f_copy(slot, 1 - core).wait_recv()
-
-    each_peer(f_wait)
-    weigh(1 - core)
+    weigh(far)
+
+    def f_wait(way, h):
+        def step(d):
+            slot = (c + n_ctx - d) % n_ctx
+            f_copy(way, slot, h, sib).wait_recv()
+
+        return step
+
+    each_peer(f_wait(1, sib))
+    weigh(sib)
+    each_peer(f_wait(2, far_sib))
+    weigh(far_sib)
 
     for cp in to_far + to_sib + fwd:
         cp.wait_send()
@@ -724,7 +792,9 @@
 
     def sent(d):
         slot = (c + n_ctx - d) % n_ctx
-        f_copy(slot, core).wait_send()
+        f_copy(0, slot, t, far).wait_send()
+        f_copy(1, slot, t, sib).wait_send()
+        f_copy(2, slot, far, sib).wait_send()
         e_copy(d).wait_send()
         r_copy(d).wait_send()
         g_copy(d).wait_send()
@@ -732,6 +802,21 @@
     each_peer(sent)
     for cp in m_sib + [m_far]:
         cp.wait_send()
+
+
+def hand_over(*refs):
+    count = len(refs) // 3
+    ins, outs, held = refs[:count], refs[count : 2 * count], refs[2 * count : 3 * count]
+    in_sem, out_sem = refs[3 * count :]
+    loads = [pltpu.make_async_copy(ins[k], held[k], in_sem.at[k]) for k in range(count)]
+    stores = [pltpu.make_async_copy(held[k], outs[k], out_sem.at[k]) for k in range(count)]
+    for cp in loads:
+        cp.start()
+    for k in range(count):
+        loads[k].wait()
+        stores[k].start()
+    for cp in stores:
+        cp.wait()
 
 
 def fused_body(
@@ -743,21 +828,8 @@
     steps = n_rows // SUB
     block = feats * n_tp // n_ctx
     per = n_ctx // n_tp
-    rate = jnp.exp(log_decay)
-    fac = jnp.sqrt(-jnp.expm1(-2.0 * rate))
-    tables = jnp.concatenate(
-        [
-            jnp.exp(-rate),
-            jnp.exp(-rate * steps),
-            jnp.exp(-rate * n_rows),
-            residues * fac,
-            rate,
-            fac,
-            rate * residues * jnp.exp(-2.0 * rate) / fac,
-            rate * residues * fac,
-        ],
-        axis=0,
-    )
+    whole = pl.BlockSpec(memory_space=pl.ANY)
+    hbm = pl.BlockSpec(memory_space=pltpu.HBM)
     vmem = pl.BlockSpec(memory_space=pltpu.VMEM)
     dma = pltpu.SemaphoreType.DMA
     outs = pl.pallas_call(
@@ -772,12 +844,18 @@
             jax.ShapeDtypeStruct((modes, chans), F32),
             jax.ShapeDtypeStruct((modes, chans), F32),
         ),
-        in_specs=[vmem] * 5 + [pl.BlockSpec(memory_space=pl.ANY), vmem],
+        in_specs=[hbm] * 8,
         out_specs=(vmem,) * 8,
         scratch_shapes=[
+            pltpu.VMEM((n_rows, chans), BF16),
+            pltpu.VMEM((n_rows, chans), BF16),
+            pltpu.VMEM((n_rows, chans), BF16),
+            pltpu.VMEM((2, modes, chans), F32),
+            pltpu.VMEM((1, chans), F32),
+            pltpu.VMEM((8 * modes, chans), F32),
             pltpu.VMEM(out_weight.shape, BF16),
             pltpu.VMEM((n_tp, n_rows, feats), BF16),
-            pltpu.VMEM((2, n_ctx, n_rows, block // 2), BF16),
+            pltpu.VMEM((n_tp, n_ctx, n_rows, block // n_tp), BF16),
             pltpu.VMEM((n_ctx, n_rows, chans), BF16),
             pltpu.VMEM((n_ctx, 2 * modes, chans), BF16),
             pltpu.VMEM((n_ctx, 4 * modes, chans), BF16),
@@ -797,13 +875,14 @@
             pltpu.VMEM((4 * modes, chans), F32),
             pltpu.VMEM((modes, SUB, chans), F32),
             pltpu.VMEM((modes, SUB, chans), F32),
+            dma((7,)),
             dma,
             dma((3, per)),
             dma((3, per)),
             dma((2, per, 2)),
             dma((n_ctx,)),
-            dma((n_ctx,)),
-            dma((n_ctx,)),
+            dma((3, n_ctx)),
+            dma((3, n_ctx)),
             dma((n_ctx,)),
             dma((n_ctx,)),
             dma((n_ctx,)),
@@ -814,9 +893,19 @@
             dma((3,)),
         ],
         compiler_params=pltpu.CompilerParams(
-            collective_id=0, has_side_effects=True, vmem_limit_bytes=48 * 2**20
+            collective_id=0, has_side_effects=True, vmem_limit_bytes=60 * 2**20
         ),
-    )(outer_gate, inner_gate, values, tables, skip_gain[None, :], out_weight, out_grad)
+    )(
+        outer_gate, inner_gate, values, residues, log_decay, skip_gain[None, :], out_weight, out_grad
+    )
+    outs = pl.pallas_call(
+        hand_over,
+        out_shape=tuple(jax.ShapeDtypeStruct(o.shape, o.dtype) for o in outs),
+        in_specs=[whole] * 8,
+        out_specs=(whole,) * 8,
+        scratch_shapes=[pltpu.VMEM(o.shape, o.dtype) for o in outs] + [dma((8,)), dma((8,))],
+        compiler_params=pltpu.CompilerParams(vmem_limit_bytes=60 * 2**20),
+    )(*outs)
     return outs[:5] + (outs[5][0],) + outs[6:]
 
 
@@ -824,7 +913,7 @@
     n_rows = arrays[0].shape[0]
     feats = arrays[-1].shape[1]
     modes = arrays[3].shape[0]
-    pairs = n_tp == 4 and n_ctx % n_tp == 0 and (feats * n_tp // n_ctx) % 256 == 0
+    pairs = n_tp == 4 and n_ctx % n_tp == 0 and (feats * n_tp // n_ctx) % (128 * n_tp) == 0
     if pairs and n_rows % 16 == 0 and modes % 16 == 0:
         return fused_body(n_ctx, n_tp, *arrays)
     return spectral_body(*arrays)

time: 82.4 us -> 60.4 us (0.73)
  the two profiles are of different devices: /device:TPU:25 before, /device:TPU:23 now
where the time goes in v2:
time: 60.4 us; the launch traced here: 60.2 us
  Pallas kernels  59.5 us (99%)
  between operations  0.64 us (1%)
    pallas_call x1, Pallas kernels, fused_body(): pl.pallas_call(functools.partial(fused_kernel, n_ctx, n_tp), out_shape=(j...  57 us
    pallas_call x1, Pallas kernels, fused_body(): pl.pallas_call(hand_over, out_shape=tuple((jax.ShapeDtypeStruct(o.shape,...  2.57 us

profile of v2, /device:TPU:23, one launch (start us, length us, event | category | flops | bytes accessed | tf_op | source)
XLA Modules:
  0.0 60.2 jit_solution(15761807439389765243)
XLA Ops:
  0.6 57.0 %shard_map.143 = (bf16[128,2048]{1,0:T(8,128)(2,1)}, bf16[128,256]{1,0:T(8,128)(2,1)}, bf16[128,256]{1,0:T(8,128)(2,1)}, bf16[128,256]{1,0:T(8,128)(2,1)}, f32[2...) custom-call(bf16[128,256]{1,0:T(8,128)(2,1)} %outer_hbm.1, ...), custom_call_target="tpu_custom_call" | custom-call | tf_op jit(solution)/shard_map/pallas_call | solution.py:835
  57.6 2.6 %shard_map.144 = (bf16[128,2048]{1,0:T(8,128)(2,1)}, bf16[128,256]{1,0:T(8,128)(2,1)}, bf16[128,256]{1,0:T(8,128)(2,1)}, bf16[128,256]{1,0:T(8,128)(2,1)}, f32[2...) custom-call(bf16[128,2048]{1,0:T(8,128)(2,1)} %get-tuple-element.24.refs_0_, ...), custom_call_target="tpu_custom_call" | custom-call | tf_op jit(solution)/shard_map/pallas_call | solution.py:901
